TPU v7x, 256 devices: a whole 4x4x8 slice. The times are simulated.
256 devices in a mesh: member: 64 (over z, x, core), dp: 4 (over y).
Axes of the slice: x: 4, y: 4, z: 8, core: 2. Of those that a mesh axis runs over, the one named last changes fastest.
Arguments:
- feature_pool: bfloat16 [2048, 256], P('dp'), may hold values from -6 to 6
- labels: int32 [2048], P('dp'), may hold values from 0 to 9
- sample_rows: int32 [1024], P('dp'), may hold values from 0 to 511
- noise_variance: float32 [10], replicated, may hold values from 20 to 80
- first_weight: bfloat16 [128, 256, 2048], P('member', None, 'dp'), may hold values from -6 to 6
- middle_weight: bfloat16 [128, 2048, 2048], P('member', 'dp'), may hold values from -6 to 6
- last_weight: bfloat16 [128, 2048, 10], P('member', 'dp'), may hold values from -6 to 6
Outputs:
- new_first: bfloat16 [128, 256, 2048], P('member', None, 'dp')
- new_middle: bfloat16 [128, 2048, 2048], P('member', 'dp')
- new_last: bfloat16 [128, 2048, 10], P('member', 'dp')
Inputs may be any that keep to these rules, and one draw needn't show every extreme that they name: Sample i reads pool row (i // 256) * 512 + sample_rows[i]. `labels`: class index of each pool row.
All inputs are finite; a program needn't handle non-finite values.
Results may differ from a plain program's by a relative error of at most 0.013.
Values may be sent and summed in bfloat16 or wider, within the bound.
A program may use at most 128 MiB of HBM per device.

v0:
```python
import jax
import jax.numpy as jnp
from jax import lax
from jax.sharding import PartitionSpec as P

F_IN = 256
H = 2048


precise = lax.Precision.HIGHEST


def from_everyone(x, axis):
    size = lax.axis_size(axis)
    return lax.all_to_all(jnp.broadcast_to(x[None], (size, *x.shape)), axis, 0, 0, tiled=True)


def in_order(parts, dim):
    shape = list(parts.shape[1:])
    shape[dim] *= parts.shape[0]
    return jnp.moveaxis(parts, 0, dim).reshape(shape)


def gathered_copies(x, axis, dim):
    parts = from_everyone(x, axis)
    return in_order(parts, dim)


def side_by_side(arrays, axis, split_dim, concat_dim, along):
    widths = [a.shape[along] for a in arrays]
    both = jnp.concatenate(arrays, axis=along)
    filled = lax.all_to_all(both, axis, split_axis=split_dim, concat_axis=concat_dim, tiled=True)
    return tuple(jnp.split(filled, [sum(widths[:k]) for k in range(1, len(widths))], axis=along))


def update_piece(piece, mixing):
    ensemble = piece.shape[0]
    flat = piece.reshape(ensemble, -1)
    upper = mixing.astype(jnp.bfloat16)
    lower = (mixing - upper.astype(jnp.float32)).astype(jnp.bfloat16)
    stacked = jnp.concatenate([upper.T, lower.T], axis=0)
    both = jnp.dot(stacked, flat, preferred_element_type=jnp.float32)
    product = both[:ensemble] + both[ensemble:]
    column_total = jnp.sum(mixing, axis=0)
    average = jnp.sum(flat, axis=0, dtype=jnp.float32) / ensemble
    renewed = flat.astype(jnp.float32) + product - column_total[:, None] * average[None, :]
    return renewed.astype(jnp.bfloat16).reshape(piece.shape)


def on_device(
    feature_pool, labels, sample_rows, noise_variance, first_weight, middle_weight, last_weight
):
    local_count = sample_rows.shape[0]
    members_here = first_weight.shape[0]
    classes_total = noise_variance.shape[0]
    in_scale = F_IN ** (-0.5)
    hid_scale = H ** (-0.5)
    inputs = feature_pool[sample_rows]
    classes = labels[sample_rows]
    target = (classes[:, None] == jnp.arange(classes_total, dtype=jnp.int32)[None, :]).astype(
        jnp.float32
    )
    window = gathered_copies(inputs, "dp", 0)
    hidden_one = jnp.tanh(
        jnp.einsum("sf,jfh->jsh", window, first_weight, preferred_element_type=jnp.float32)
        * in_scale
    ).astype(jnp.bfloat16)
    term = jnp.einsum("jsk,jkh->sjh", hidden_one, middle_weight, preferred_element_type=jnp.float32)
    summed = lax.psum_scatter(
        term.reshape(lax.axis_size("dp") * local_count, members_here * H).astype(jnp.bfloat16),
        "dp",
        scatter_dimension=0,
        tiled=True,
    ).astype(jnp.float32)
    hidden_two = jnp.tanh(summed.reshape(local_count, members_here, H) * hid_scale).astype(
        jnp.bfloat16
    )
    last_full = lax.all_gather(last_weight, "dp", axis=1, tiled=True)
    outputs = (
        jnp.einsum("sjh,jhc->jsc", hidden_two, last_full, preferred_element_type=jnp.float32)
        * hid_scale
    )
    whiten = 1.0 / jnp.sqrt(noise_variance)
    scaled = (outputs * whiten).reshape(members_here, local_count * classes_total)
    observed = (target * whiten).reshape(local_count * classes_total)
    every_member = lax.all_gather(scaled, "member", axis=0, tiled=True)
    center = jnp.mean(every_member, axis=0)
    anomaly = every_member - center
    gram_part = jnp.dot(anomaly, anomaly.T, precision=precise)
    drive_part = jnp.dot(anomaly, observed - center, precision=precise)
    gram_matrix, drive = (
        lax.psum(gram_part.astype(jnp.bfloat16), "dp").astype(jnp.float32),
        lax.psum(drive_part.astype(jnp.bfloat16), "dp").astype(jnp.float32),
    )
    ensemble = gram_matrix.shape[0]
    system = gram_matrix + ensemble * jnp.eye(ensemble, dtype=jnp.float32)
    factor = jnp.linalg.cholesky(system)
    mixing = jax.scipy.linalg.cho_solve((factor, True), drive[:, None] - gram_matrix)
    grouped = (
        lax.all_to_all(first_weight, "member", split_axis=1, concat_axis=0, tiled=True),
        *side_by_side((middle_weight, last_weight), "member", 1, 0, 2),
    )
    updated = (
        update_piece(grouped[0], mixing),
        update_piece(grouped[1], mixing),
        update_piece(grouped[2], mixing),
    )
    new_first, new_middle, new_last = (
        lax.all_to_all(updated[0], "member", split_axis=0, concat_axis=1, tiled=True),
        *side_by_side((updated[1], updated[2]), "member", 0, 1, 2),
    )
    return (new_first, new_middle, new_last)


def solution(mesh):
    in_specs = (
        P("dp", None),
        P("dp"),
        P("dp"),
        P(),
        P("member", None, "dp"),
        P("member", "dp", None),
        P("member", "dp", None),
    )
    out_specs = (P("member", None, "dp"), P("member", "dp", None), P("member", "dp", None))
    return jax.shard_map(
        on_device, mesh=mesh, in_specs=in_specs, out_specs=out_specs, check_vma=False
    )
```

profile of v0, /device:TPU:1, one launch (start us, length us, event | category | flops | bytes accessed | tf_op | source)
XLA Modules:
  0.0 415.9 jit_solution(17062474247449413385)
XLA Ops:
  7.2 0.7 compare_select_fusion
  8.1 1.1 gather_fusion
  9.3 13.4 %all_to_all.74 = bf16[4,256,256]{2,1,0:T(8,128)(2,1)S(1)} all-to-all(bf16[4,256,256]{2,1,0:T(8,128)(2,1)S(1)} %broadcast_in_dim.6), channel_id=1, replica_groups=mesh['member'=64,'dp'=4] {'dp'}, dimensions={0} | all-to-all | bytes 1048576 | tf_op jit(solution)/shard_map/all_to_all | solution.py:15
  22.7 9.5 %convert_bitcast_fusion = bf16[1024,2,2048]{2,0,1:T(8,128)(2,1)} fusion(bf16[2,512,2048]{2,1,0:T(8,128)(2,1)} %param.12, bf16[1024,256,1]{1,0,2:T(8,128)(2,1)S(1)} %bitcast.96, bf16[2,256,512]{2,1,0:T(8,128)(2,1)} %param.11), kind=kOutput, calls=%fused_computation.7 | convolution fusion | flops 4838129664 | bytes 13631488 | tf_op jit(solution)/shard_map/jsk,jkh->sjh/dot_general | solution.py:68
  32.2 11.9 %copy.78 = bf16[1024,2,2048]{0,2,1:T(8,128)(2,1)} copy(bf16[1024,2,2048]{2,0,1:T(8,128)(2,1)} %convert_bitcast_fusion) | data formatting | bytes 16777216 | tf_op jit(solution)/shard_map/convert_element_type | solution.py:70
  44.0 1.0 copy-done.5
  45.1 1.3 copy.76
  46.4 14.0 %all-to-all-start = ((bf16[2,256,512]{2,0,1:T(2,128)(2,1)}), bf16[2,256,512]{2,0,1:T(2,128)(2,1)S(1)}, u32[]{:S(2)}, u32[]{:S(2)}) async-start(bf16[2,256,512]{2,0,1:T(2,128)(2,1)} %copy.76), calls=%async_computation | async-start | bytes 1048576 | tf_op jit(solution)/shard_map/all_to_all | solution.py:100
  60.4 8.5 %copy.84 = bf16[2,512,2048]{2,0,1:T(2,128)(2,1)} copy(bf16[2,512,2048]{2,1,0:T(8,128)(2,1)} %param.12) | data formatting | bytes 8388608 | tf_op args[5]
  69.1 8.4 %pad_maximum_fusion = bf16[2,512,2058]{2,0,1:T(2,128)(2,1)} fusion(bf16[2,512,10]{2,0,1:T(2,128)(2,1)S(1)} %copy.85, bf16[2,512,2048]{2,0,1:T(2,128)(2,1)} %copy.84), kind=kLoop, calls=%fused_computation.8 | loop fusion | flops 8429568 | bytes 8429568 | tf_op jit(solution)/shard_map/concatenate | solution.py:31
  77.6 0.4 all-to-all-done
  78.0 10.1 %all-to-all-start.3 = ((bf16[2,512,2058]{2,0,1:T(2,128)(2,1)}), bf16[2,512,2058]{2,0,1:T(2,128)(2,1)}, u32[]{:S(2)}, u32[]{:S(2)}) async-start(bf16[2,512,2058]{2,0,1:T(2,128)(2,1)} %pad_maximum_fusion), calls=%async_computation.4 | async-start | bytes 8912896 | tf_op jit(solution)/shard_map/all_to_all | solution.py:32
  88.2 11.1 %all_gather.6 = bf16[2,2048,10]{1,2,0:T(8,128)(2,1)S(1)} all-gather(bf16[2,512,10]{1,2,0:T(8,128)(2,1)S(1)} %copy.79), channel_id=1, replica_groups=mesh['member'=64,'dp'=4] {'dp'}, dimensions={1}, use_global_device_ids=true | all-gather | bytes 102400 | tf_op jit(solution)/shard_map/all_gather | solution.py:78
  99.3 31.2 %reduce-scatter.2.cloned.1.call-done = bf16[256,4096]{0,1:T(8,128)(2,1)} async-done(((bf16[1024,4096]{0,1:T(8,128)(2,1)}), bf16[256,4096]{0,1:T(8,128)(2,1)}) %reduce-scatter.2.cloned.1.call-update) | async-done | bytes 2097168 | tf_op jit(solution)/shard_map/reduce_scatter | solution.py:69
  130.5 2.1 tanh_convert_fusion
  132.7 0.3 convolution_multiply_fusion
  133.2 0.8 reshape.120
  134.0 1.9 gather_fusion.1
  136.9 51.8 %all-to-all-done.3 = bf16[2,512,2058]{2,0,1:T(2,128)(2,1)} async-done(((bf16[2,512,2058]{2,0,1:T(2,128)(2,1)}), bf16[2,512,2058]{2,0,1:T(2,128)(2,1)}, u32[]{:S(2)}, u32[]{:S(2)}) %all-to-all-start.3) | async-done | bytes 4214816 | tf_op jit(solution)/shard_map/all_to_all | solution.py:32
  188.6 2.9 copy.86
  191.6 3.0 split.16
  194.6 0.4 copy-done.3
  195.2 2.9 convert_reduce_fusion
  198.3 7.3 %copy.95 = bf16[16,8,8,2048]{3,1,2,0:T(8,128)(2,1)} copy(bf16[16,8,8,2048]{3,2,1,0:T(8,128)(2,1)} %bitcast.85) | data formatting | bytes 8388608
  205.7 14.3 %all-gather.3.cloned.1.call-done = f32[64,2,2560]{2,1,0:T(2,128)} async-done(((f32[1,2,2560]{2,1,0:T(2,128)}), f32[64,2,2560]{2,1,0:T(2,128)}) %all-gather.3.cloned.1.call-update) | async-done | bytes 1310736 | tf_op jit(solution)/shard_map/all_gather | solution.py:86
  220.0 1.7 reduce_sum.43
  221.8 2.2 reshape.121
  224.0 1.2 fusion.8
  225.2 1.1 fusion.14
  226.3 13.8 %all-reduce = (bf16[128,128]{1,0:T(8,128)(2,1)S(1)}, bf16[128]{0:T(256)(128)(2,1)S(1)}) all-reduce(bf16[128,128]{1,0:T(8,128)(2,1)S(1)} %fusion.8, bf16[128]{0:T(256)(128)(2,1)S(1)} %fusion.14), channel_id=1, replica_groups=mesh['member'=64,'dp'=4] {'dp'}, use_global_device_ids=true, to_apply=%region_2.0 | all-reduce | flops 16512 | bytes 66048 | tf_op jit(solution)/shard_map/psum | solution.py:92
  240.3 11.7 %cholesky.16 = f32[128,128]{1,0:T(8,128)S(1)} custom-call(f32[128,128]{1,0:T(8,128)S(1)} %fusion.29), custom_call_target="Cholesky" | custom-call | tf_op jit(solution)/shard_map/jit(cholesky)/cholesky | solution.py:97
  252.0 0.6 compare_reduce_fusion
  252.6 0.7 fusion.23
  253.3 9.8 %custom-call.10 = f32[1,128,128]{1,2,0:T(8,128)S(1)} custom-call(f32[1,128,128]{2,1,0:T(8,128)S(1)} %fusion.23), custom_call_target="InvertDiagBlocksLowerTriangular" | custom-call | tf_op jit(solution)/shard_map/jit(_cho_solve)/triangular_solve | solution.py:98
  263.7 0.4 fusion.36
  264.5 1.2 reshape.97
  265.6 10.8 %all-to-all-start.2 = ((bf16[128,4,512]{2,1,0:T(4,128)(2,1)}), bf16[128,4,512]{2,1,0:T(4,128)(2,1)S(1)}, u32[]{:S(2)}, u32[]{:S(2)}) async-start(bf16[128,4,512]{2,1,0:T(4,128)(2,1)} %reshape.97), calls=%async_computation.3 | async-start | bytes 1048576 | tf_op jit(solution)/shard_map/all_to_all | solution.py:109
  276.5 4.7 %fusion.35 = f32[256,16384]{1,0:T(8,128)S(1)} fusion(bf16[128,16384]{1,0:T(8,128)(2,1)} %bitcast.80, bf16[128,128]{0,1:T(8,128)(2,1)S(1)} %get-tuple-element.29, bf16[128,128]{0,1:T(8,128)(2,1)S(1)} %get-tuple-element.24), kind=kOutput, calls=%fused_computation.57 | convolution fusion | flops 1073872896 | bytes 21037056 | tf_op jit(solution)/shard_map/dot_general | solution.py:42
  281.2 3.3 fusion.2
  285.1 5.0 %copy.97 = bf16[16,8,8,2048]{3,2,1,0:T(8,128)(2,1)S(1)} copy(bf16[16,8,8,2048]{3,1,2,0:T(8,128)(2,1)} %bitcast.87) | data formatting | bytes 8388608
  290.1 2.5 pad_maximum_fusion.1
  292.6 1.5 all-to-all-done.2
  294.1 9.0 %all-to-all-start.4 = ((bf16[128,8,2058]{2,1,0:T(8,128)(2,1)}), bf16[128,8,2058]{2,1,0:T(8,128)(2,1)}, u32[]{:S(2)}, u32[]{:S(2)}) async-start(bf16[128,8,2058]{2,1,0:T(8,128)(2,1)} %pad_maximum_fusion.1), calls=%async_computation.5 | async-start | bytes 8912896 | tf_op jit(solution)/shard_map/all_to_all | solution.py:32
  303.2 0.9 all_to_all.60
  304.2 98.6 %all-to-all-done.4 = bf16[128,8,2058]{2,1,0:T(8,128)(2,1)} async-done(((bf16[128,8,2058]{2,1,0:T(8,128)(2,1)}), bf16[128,8,2058]{2,1,0:T(8,128)(2,1)}, u32[]{:S(2)}, u32[]{:S(2)}) %all-to-all-start.4) | async-done | bytes 4214816 | tf_op jit(solution)/shard_map/all_to_all | solution.py:32
  402.8 2.6 copy.101
  405.4 2.6 split.18
  408.0 0.8 copy.90
  (56 shorter events, 3.9 us)
Async XLA Ops:
  7.2 1.0 copy-start
  7.2 123.3 %reduce-scatter.2.cloned.1.call-start = ((), (), s32[]{:S(2)}) async-start(), calls=%async_computation.6 | async-start | bytes 10485760 | tf_op jit(solution)/shard_map/reduce_scatter | solution.py:69
  44.0 1.0 copy-start.5
  46.4 31.6 %all-to-all-start = ((bf16[2,256,512]{2,0,1:T(2,128)(2,1)}), bf16[2,256,512]{2,0,1:T(2,128)(2,1)S(1)}, u32[]{:S(2)}, u32[]{:S(2)}) async-start(bf16[2,256,512]{2,0,1:T(2,128)(2,1)} %copy.76), calls=%async_computation | async-start | bytes 1048576 | tf_op jit(solution)/shard_map/all_to_all | solution.py:100
  60.4 8.5 %copy-start.6 = (bf16[2,512,10]{1,0,2:T(2,128)(2,1)S(1)}, bf16[2,512,10]{1,0,2:T(2,128)(2,1)}, u32[]{:S(2)}) copy-start(bf16[2,512,10]{1,0,2:T(2,128)(2,1)} %param.13) | copy-start | bytes 61444
  77.6 21.7 %copy-start.7 = (f32[10]{0:T(128)S(1)}, f32[10]{0:T(128)}, u32[]{:S(2)}) copy-start(f32[10]{0:T(128)} %param.10) | copy-start | bytes 124
  78.0 110.7 %all-to-all-start.3 = ((bf16[2,512,2058]{2,0,1:T(2,128)(2,1)}), bf16[2,512,2058]{2,0,1:T(2,128)(2,1)}, u32[]{:S(2)}, u32[]{:S(2)}) async-start(bf16[2,512,2058]{2,0,1:T(2,128)(2,1)} %pad_maximum_fusion), calls=%async_computation.4 | async-start | bytes 8912896 | tf_op jit(solution)/shard_map/all_to_all | solution.py:32
  88.1 45.9 %copy-start.2 = (s32[512]{0:T(512)S(1)}, s32[512]{0:T(512)}, u32[]{:S(2)}) copy-start(s32[512]{0:T(512)} %param.8) | copy-start | bytes 6148
  88.1 131.9 %all-gather.3.cloned.1.call-start = ((), (), s32[]{:S(2)}) async-start(), calls=%async_computation.7 | async-start | bytes 1331200 | tf_op jit(solution)/shard_map/all_gather | solution.py:86
  191.6 3.4 copy-start.3
  265.6 28.4 %all-to-all-start.2 = ((bf16[128,4,512]{2,1,0:T(4,128)(2,1)}), bf16[128,4,512]{2,1,0:T(4,128)(2,1)S(1)}, u32[]{:S(2)}, u32[]{:S(2)}) async-start(bf16[128,4,512]{2,1,0:T(4,128)(2,1)} %reshape.97), calls=%async_computation.3 | async-start | bytes 1048576 | tf_op jit(solution)/shard_map/all_to_all | solution.py:109
  276.5 4.7 %copy-start.4 = (bf16[16,8,8,2048]{3,1,2,0:T(8,128)(2,1)S(1)}, bf16[16,8,8,2048]{3,1,2,0:T(8,128)(2,1)}, u32[]{:S(2)}) copy-start(bf16[16,8,8,2048]{3,1,2,0:T(8,128)(2,1)} %copy.95) | copy-start | bytes 12582916
  294.1 108.7 %all-to-all-start.4 = ((bf16[128,8,2058]{2,1,0:T(8,128)(2,1)}), bf16[128,8,2058]{2,1,0:T(8,128)(2,1)}, u32[]{:S(2)}, u32[]{:S(2)}) async-start(bf16[128,8,2058]{2,1,0:T(8,128)(2,1)} %pad_maximum_fusion.1), calls=%async_computation.5 | async-start | bytes 8912896 | tf_op jit(solution)/shard_map/all_to_all | solution.py:32
  405.4 3.4 copy-start.1
Sparse Core Ops, SparseCore 0:
  44.2 86.3 reduce-scatter.1
  134.1 85.8 all-gather.2
where the time goes:
time: 422 us; the launch traced here: 416 us
  waiting for transfers between devices  198 us (47%)
  local copies, waits for them, and re-layouts  57.4 us (14%)
  other arithmetic  45.7 us (11%)
  starting transfers between devices  44 us (10%)
  blocking collectives  38.3 us (9%)
  matrix products  18 us (4%)
  between operations  14.7 us (3%)
    all_to_all x2, waiting for transfers between devices, side_by_side(): lax.all_to_all(both, axis, split_axis=split_dim, concat_axis=concat_dim,...  150 us
    reduce_scatter x1, waiting for transfers between devices, on_device(): lax.psum_scatter(term.reshape(lax.axis_size('dp') * local_count, members_...  31.2 us
    unnamed x28, local copies, waits for them, and re-layouts  27.9 us
    all_to_all x2, starting transfers between devices, side_by_side(): lax.all_to_all(both, axis, split_axis=split_dim, concat_axis=concat_dim,...  19.1 us
    all_gather x1, waiting for transfers between devices, on_device(): every_member = lax.all_gather(scaled, 'member', axis=0, tiled=True)  14.3 us
    all_to_all x1, starting transfers between devices, on_device(): lax.all_to_all(first_weight, 'member', split_axis=1, concat_axis=0, tiled...  14 us
    psum x1, blocking collectives, on_device(): lax.psum(gram_part.astype(jnp.bfloat16), 'dp').astype(jnp.float32)  13.8 us
    all_to_all x1, blocking collectives, from_everyone(): lax.all_to_all(jnp.broadcast_to(x[None], (size, *x.shape)), axis, 0, 0, t...  13.4 us
  transfers between devices with their start and end apart: 6, of which 6 were waited for; matrix products, arithmetic and copies ran while one was open for 14% of the time, Pallas kernels for 0%

commit v1 on v0

v1 whole, which is shorter than its diff:
```python
import functools

import jax
import jax.numpy as jnp
from jax import lax
from jax.experimental import pallas as pl
from jax.experimental.pallas import tpu as pltpu
from jax.sharding import PartitionSpec as P

F_IN = 256
H = 2048
MESH = pl.DeviceIdType.MESH
NM = 64
ND = 4
ENS = 128
TILE = 16
WIDE = 1024
SLIM = 128
LAST_TILES = 3
ROWS = 24
LAST_OWNERS = (3, 28, 53)
VMEM_LIMIT = 60 * 1024 * 1024


def middle_block(p):
    return pl.ds(pl.multiple_of((p // 2) * TILE, TILE), TILE), pl.ds(pl.multiple_of((p % 2) * WIDE, WIDE), WIDE)


def first_block(p):
    return pl.ds(pl.multiple_of((p // 4) * TILE, TILE), TILE), pl.ds(pl.multiple_of((p % 4) * SLIM, SLIM), SLIM)


def pair(p):
    return pl.ds(pl.multiple_of(2 * p, 2), 2)


def plane_peer(me, step):
    z, low = me // 8, me % 8
    plane, within = step // 8, step % 8
    return ((z + plane) % 8) * 8 + (low + within) % 8


def spd_inverse(system):
    size = system.shape[0]
    group = 8
    sub = lax.broadcasted_iota(jnp.int32, (group, size), 0)
    lane = lax.broadcasted_iota(jnp.int32, (group, size), 1)
    lanes = lax.broadcasted_iota(jnp.int32, (size - group, size), 1)

    def one_round(_, a):
        panel = a[:group, :]
        for k in range(group):
            row = panel[k:k + 1, :]
            col = panel[:, k:k + 1]
            pivot = 1.0 / row[:, k:k + 1]
            row = jnp.where(lane[:1] == k, pivot, row * pivot)
            panel = jnp.where(sub == k, row, jnp.where(lane == k, 0.0, panel) - col * row)
        below = jnp.where(lanes < group, 0.0, a[group:, :])
        for k in range(group):
            below = below - a[group:, k:k + 1] * panel[k:k + 1, :]
        turned = jnp.concatenate([below, panel], axis=0)
        return pltpu.roll(turned, size - group, 1)

    return lax.fori_loop(0, size // group, one_round, system)


def member_of_slot(i):
    return (i % 8) * 16 + ((i // 8) % 4) * 4 + ((i // 32) % 2) * 2 + i // 64


def forward_kernel(
    first, middle, window, last_t, last_tiles, gain, observed,
    theta, theta_last, mix_t,
    wf, mc, xw, h1, acc, part, part_in, every, hi_part, lo_part, gram, gram_in,
    y_send, y_recv, a_send, a_recv, l_send, l_recv, p_send, p_recv, s_send, s_recv, g_send, g_recv,
):
    me, y = lax.axis_index("member"), lax.axis_index("dp")
    barrier = pltpu.get_barrier_semaphore()
    for d in range(1, ND):
        pl.semaphore_signal(barrier, inc=1, device_id=(me, (y + d) % ND), device_id_type=MESH)

    def greet(i, carry):
        pl.semaphore_signal(barrier, inc=1, device_id=((me + i) % NM, y), device_id_type=MESH)
        return carry

    lax.fori_loop(1, NM, greet, 0)
    pl.semaphore_wait(barrier, NM - 1 + ND - 1)

    def y_copies(d):
        t = (y - d) % ND
        cols = pl.ds(pl.multiple_of(t * 512, 512), 512)
        jobs = ((window, xw.at[d]), (first, wf.at[d]), (middle.at[:, :, cols], mc.at[d]))
        out = []
        for k, (src, dst) in enumerate(jobs):
            if d == 0:
                out.append(pltpu.make_async_copy(src, dst, y_recv.at[k, d]))
            else:
                out.append(
                    pltpu.make_async_remote_copy(
                        src_ref=src, dst_ref=dst, send_sem=y_send.at[k, d], recv_sem=y_recv.at[k, d],
                        device_id=(me, t), device_id_type=MESH,
                    )
                )
        return out

    ys = [y_copies(d) for d in range(ND)]
    for k in range(3):
        for d in (0, 2, 1, 3):
            ys[d][k].start()

    def exchange(p, remote):
        mr, mcol = middle_block(p)
        fr, fcol = first_block(p)
        jobs = (
            (middle.at[:, mr, mcol], theta.at[pair(me), :, pl.ds(0, WIDE)]),
            (first.at[:, fr, fcol], theta.at[pair(me), :, pl.ds(WIDE, SLIM)]),
        )
        for src, dst in jobs:
            if remote:
                pltpu.make_async_remote_copy(
                    src_ref=src, dst_ref=dst, send_sem=a_send, recv_sem=a_recv, device_id=(p, y), device_id_type=MESH
                ).start()
            else:
                pltpu.make_async_copy(src, dst, a_recv).start()

    exchange(me, False)

    def send_one(step, carry):
        exchange(plane_peer(me, step), True)
        return carry

    lax.fori_loop(1, NM, send_one, 0)
    for t, owner in enumerate(LAST_OWNERS):
        @pl.when(me == owner)
        def _():
            pltpu.make_async_copy(last_tiles.at[:, t], theta_last.at[pair(me)], l_recv).start()

        @pl.when(me != owner)
        def _():
            pltpu.make_async_remote_copy(
                src_ref=last_tiles.at[:, t], dst_ref=theta_last.at[pair(me)], send_sem=l_send.at[t], recv_sem=l_recv,
                device_id=(owner, y), device_id_type=MESH,
            ).start()

    in_scale = F_IN ** (-0.5)
    hid_scale = H ** (-0.5)
    order = (0, 1, 3, 2)
    for k in (0, 1):
        for d in order:
            if d == 0:
                ys[d][k].wait()
            else:
                ys[d][k].wait_recv()

    for d in order:
        for m in range(2):
            def rows_one(i, carry, d=d, m=m):
                rows = pl.ds(pl.multiple_of(i * 256, 256), 256)
                z = jnp.dot(xw[i], wf[d, m], preferred_element_type=jnp.float32)
                h1[m, d, rows, :] = jnp.tanh(z * in_scale).astype(jnp.bfloat16)
                return carry

            lax.fori_loop(0, 4, rows_one, 0)
    for n, d in enumerate(order):
        if d == 0:
            ys[d][2].wait()
        else:
            ys[d][2].wait_recv()
        for m in range(2):
            def rows_two(i, carry, d=d, m=m, n=n):
                rows = pl.ds(pl.multiple_of(i * 256, 256), 256)
                z = jnp.dot(h1[m, d, rows, :], mc[d, m], preferred_element_type=jnp.float32)
                if n == 0:
                    acc[m, rows, :] = z
                elif n < ND - 1:
                    acc[m, rows, :] += z
                else:
                    h2 = jnp.tanh((acc[m, rows, :] + z) * hid_scale).astype(jnp.bfloat16)
                    here = lax.dot_general(
                        last_t[m], h2, (((1,), (1,)), ((), ())), preferred_element_type=jnp.float32
                    )
                    if m == 0:
                        part[i] = here
                    else:
                        part[i] += here
                return carry

            lax.fori_loop(0, 4, rows_two, 0)

    def part_copy(d):
        t = (y - d) % ND
        return pltpu.make_async_remote_copy(
            src_ref=part.at[(ND - d) % ND], dst_ref=part_in.at[d], send_sem=p_send.at[d], recv_sem=p_recv.at[d],
            device_id=(me, t), device_id_type=MESH,
        )

    ps = [part_copy(d) for d in range(1, ND)]
    for c in ps:
        c.start()
    for c in ps:
        c.wait_recv()
    total = part[0] + part_in[1] + part_in[2] + part_in[3]
    z, x, core = me // 8, (me // 2) % 4, me % 2

    every[core * 32 + x * 8 + z] = (total * hid_scale) * gain[:, 0:1]

    def spread(phase, first_slot, count, p):
        slots = every.at[pl.ds(first_slot, count)]
        return pltpu.make_async_remote_copy(
            src_ref=slots, dst_ref=slots, send_sem=s_send.at[phase], recv_sem=s_recv.at[phase],
            device_id=(p, y), device_id_type=MESH,
        )

    def whole_wait(sem, count):
        slots = every.at[pl.ds(0, count)]
        pltpu.make_async_copy(slots, slots, sem).wait()

    for i in range(1, 8):
        spread(0, core * 32 + x * 8 + z, 1, ((z + i) % 8) * 8 + x * 2 + core).start()
    whole_wait(s_recv.at[0], 7)
    for i in (2, 1, 3):
        spread(1, core * 32 + x * 8, 8, z * 8 + ((x + i) % 4) * 2 + core).start()
    whole_wait(s_recv.at[1], 24)
    spread(2, core * 32, 32, z * 8 + x * 2 + 1 - core).start()
    whole_wait(s_recv.at[2], 32)

    pull = jnp.zeros((ENS, 256), jnp.float32)
    for c in range(10):
        values = jnp.concatenate([every[:, c, :], every[:, 10 + c, :]], axis=0)
        center = jnp.mean(values, axis=0, keepdims=True)
        anomaly = values - center
        upper = anomaly.astype(jnp.bfloat16)
        hi_part[:, c * 256:(c + 1) * 256] = upper
        lo_part[:, c * 256:(c + 1) * 256] = (anomaly - upper.astype(jnp.float32)).astype(jnp.bfloat16)
        pull = pull + anomaly * (observed[c:c + 1, :] - center)
    over_samples = (((1,), (1,)), ((), ()))
    squares = lax.dot_general(hi_part[...], hi_part[...], over_samples, preferred_element_type=jnp.float32)
    crossed = lax.dot_general(hi_part[...], lo_part[...], over_samples, preferred_element_type=jnp.float32)
    gram[:ENS, :] = squares + (crossed + crossed.T)
    drive_tall = jnp.broadcast_to(jnp.sum(pull, axis=1, keepdims=True), (ENS, ENS))
    gram[ENS:, :] = drive_tall.T[:8, :]

    def gram_copy(d):
        return pltpu.make_async_remote_copy(
            src_ref=gram, dst_ref=gram_in.at[d - 1], send_sem=g_send.at[d], recv_sem=g_recv.at[d],
            device_id=(me, (y - d) % ND), device_id_type=MESH,
        )

    gs = [gram_copy(d) for d in range(1, ND)]
    for c in gs:
        c.start()
    for c in gs:
        c.wait_recv()
    summed = gram[...] + gram_in[0] + gram_in[1] + gram_in[2]
    diagonal = lax.broadcasted_iota(jnp.int32, (ENS, ENS), 0) == lax.broadcasted_iota(jnp.int32, (ENS, ENS), 1)
    inverse = spd_inverse(summed[:ENS] + jnp.where(diagonal, float(ENS), 0.0))
    lift = jnp.sum(inverse * summed[ENS:ENS + 1], axis=1, keepdims=True)
    mix_t[...] = (
        float(ENS) * (inverse - jnp.mean(inverse, axis=0, keepdims=True))
        + (lift - jnp.mean(lift, axis=0, keepdims=True))
        + 1.0 / ENS
    )

    for c in ps + gs:
        c.wait_send()
    whole_wait(s_send.at[0], 7)
    whole_wait(s_send.at[1], 24)
    whole_wait(s_send.at[2], 32)
    for d in range(1, ND):
        for c in ys[d]:
            c.wait_send()
    pltpu.make_async_copy(theta, theta, a_recv).wait()
    rest = theta.at[pl.ds(0, ENS - 2)]
    pltpu.make_async_copy(rest, rest, a_send).wait()
    for t, owner in enumerate(LAST_OWNERS):
        @pl.when(me == owner)
        def _():
            pltpu.make_async_copy(theta_last, theta_last, l_recv).wait()

        @pl.when(me != owner)
        def _():
            pltpu.make_async_copy(last_tiles.at[:, t], last_tiles.at[:, t], l_send.at[t]).wait()


def update_kernel(
    theta_hbm, theta_last_hbm, mix_t,
    new_first, new_middle, new_last,
    theta, theta_last, wide_hi, wide_lo, out, out_last,
    in_sem, a_send, m_recv, f_recv, l_send, l_recv,
):
    me, y = lax.axis_index("member"), lax.axis_index("dp")
    barrier = pltpu.get_barrier_semaphore()

    def greet(i, carry):
        pl.semaphore_signal(barrier, inc=1, device_id=((me + i) % NM, y), device_id_type=MESH)
        return carry

    lax.fori_loop(1, NM, greet, 0)
    is_owner = (me == LAST_OWNERS[0]) | (me == LAST_OWNERS[1]) | (me == LAST_OWNERS[2])
    load = pltpu.make_async_copy(theta_hbm, theta, in_sem.at[0])
    load.start()
    load_last = pltpu.make_async_copy(theta_last_hbm, theta_last, in_sem.at[1])
    load_last.start()

    hi = mix_t[...].astype(jnp.bfloat16)
    lo = (mix_t[...] - hi.astype(jnp.float32)).astype(jnp.bfloat16)
    size = ENS * TILE
    spread_t = (
        member_of_slot(lax.broadcasted_iota(jnp.int32, (ENS, size), 0))
        == lax.broadcasted_iota(jnp.int32, (ENS, size), 1) // TILE
    ).astype(jnp.bfloat16)
    block = 256

    def widen(i, carry):
        rows = pl.ds(pl.multiple_of(i * block, block), block)
        row_id = lax.broadcasted_iota(jnp.int32, (block, ENS), 0) + i * block
        spread = (row_id // TILE == member_of_slot(lax.broadcasted_iota(jnp.int32, (block, ENS), 1))).astype(jnp.bfloat16)
        keep = (
            lax.broadcasted_iota(jnp.int32, (block, size), 0) % TILE
            == lax.broadcasted_iota(jnp.int32, (block, size), 1) % TILE
        )
        for source, target in ((hi, wide_hi), (lo, wide_lo)):
            tall = lax.dot_general(
                spread, source, (((1,), (1,)), ((), ())), preferred_element_type=jnp.float32
            ).astype(jnp.bfloat16)
            full = jnp.dot(tall, spread_t, preferred_element_type=jnp.float32)
            target[rows, :] = jnp.where(keep, full, 0.0).astype(jnp.bfloat16)
        return carry

    lax.fori_loop(0, size // block, widen, 0)
    load.wait()
    load_last.wait()
    pl.semaphore_wait(barrier, NM - 1)

    mr, mcol = middle_block(me)
    fr, fcol = first_block(me)

    def results(p, remote):
        jobs = (
            (out.at[pair(p), :, pl.ds(0, WIDE)], new_middle.at[:, mr, mcol], m_recv),
            (out.at[pair(p), :, pl.ds(WIDE, SLIM)], new_first.at[:, fr, fcol], f_recv),
        )
        for src, dst, sem in jobs:
            if remote:
                pltpu.make_async_remote_copy(
                    src_ref=src, dst_ref=dst, send_sem=a_send, recv_sem=sem, device_id=(p, y), device_id_type=MESH
                ).start()
            else:
                pltpu.make_async_copy(src, dst, sem).start()

    def one_plane(b, carry):
        plane = (me // 8 + b) % 8
        rows = pl.ds(pl.multiple_of(plane * block, block), block)
        members = pl.ds(pl.multiple_of(plane * 16, 16), 16)
        flat = theta[...].reshape(size, WIDE + SLIM)
        z = jnp.dot(wide_hi[rows, :], flat, preferred_element_type=jnp.float32)
        z += jnp.dot(wide_lo[rows, :], flat, preferred_element_type=jnp.float32)
        out[members] = z.astype(jnp.bfloat16).reshape(16, TILE, WIDE + SLIM)

        def send_one(c, inner):
            p = plane * 8 + (me % 8 + c) % 8

            @pl.when(p != me)
            def _():
                results(p, True)

            @pl.when(p == me)
            def _():
                results(p, False)

            return inner

        lax.fori_loop(0, 8, send_one, 0)
        return carry

    lax.fori_loop(0, 8, one_plane, 0)

    @pl.when(is_owner)
    def _():
        flat = theta_last[...].reshape(size, SLIM)

        def one(i, carry):
            rows = pl.ds(pl.multiple_of(i * block, block), block)
            z = jnp.dot(wide_hi[rows, :], flat, preferred_element_type=jnp.float32)
            z += jnp.dot(wide_lo[rows, :], flat, preferred_element_type=jnp.float32)
            out_last[pl.ds(pl.multiple_of(i * 16, 16), 16)] = z.astype(jnp.bfloat16).reshape(16, TILE, SLIM)
            return carry

        lax.fori_loop(0, 8, one, 0)

    for t, owner in enumerate(LAST_OWNERS):
        @pl.when(me == owner)
        def _():
            pltpu.make_async_copy(out_last.at[pair(me)], new_last.at[:, t], l_recv).start()

            def send_last(i, carry):
                p = (me + i) % NM
                pltpu.make_async_remote_copy(
                    src_ref=out_last.at[pair(p)], dst_ref=new_last.at[:, t], send_sem=l_send, recv_sem=l_recv,
                    device_id=(p, y), device_id_type=MESH,
                ).start()
                return carry

            lax.fori_loop(1, NM, send_last, 0)
            sent = out_last.at[pl.ds(0, ENS - 2)]
            pltpu.make_async_copy(sent, sent, l_send).wait()

    pltpu.make_async_copy(new_middle, new_middle, m_recv).wait()
    pltpu.make_async_copy(new_first, new_first, f_recv).wait()
    pltpu.make_async_copy(new_last, new_last, l_recv).wait()
    rest = out.at[pl.ds(0, ENS - 2)]
    pltpu.make_async_copy(rest, rest, a_send).wait()


def on_device(
    feature_pool, labels, sample_rows, noise_variance, first_weight, middle_weight, last_weight
):
    local_count = sample_rows.shape[0]
    members_here = first_weight.shape[0]
    classes_total = noise_variance.shape[0]
    window = feature_pool[sample_rows]
    classes = labels[sample_rows]
    target = (classes[None, :] == jnp.arange(16, dtype=jnp.int32)[:, None]).astype(jnp.float32)
    whiten = 1.0 / jnp.sqrt(noise_variance)
    observed = target * jnp.pad(whiten, (0, 16 - classes_total))[:, None]
    gain = jnp.broadcast_to(jnp.pad(jnp.tile(whiten, 2), (0, ROWS - 2 * classes_total))[:, None], (ROWS, 128))
    turned = jnp.swapaxes(last_weight, 1, 2)
    last_t = jnp.stack([
        jnp.pad(turned[m], ((m * classes_total, ROWS - (m + 1) * classes_total), (0, 0))) for m in range(members_here)
    ])
    per_member = last_weight.shape[1] * classes_total
    padded = LAST_TILES * TILE * SLIM
    last_tiles = jnp.pad(last_weight.reshape(members_here, per_member), ((0, 0), (0, padded - per_member)))
    last_tiles = last_tiles.reshape(members_here, LAST_TILES, TILE, SLIM)

    anyspace = pl.BlockSpec(memory_space=pl.ANY)
    vmem = pl.BlockSpec(memory_space=pltpu.VMEM)
    bf16, f32 = jnp.bfloat16, jnp.float32
    theta, theta_last, mix_t = pl.pallas_call(
        forward_kernel,
        out_shape=(
            jax.ShapeDtypeStruct((ENS, TILE, WIDE + SLIM), bf16),
            jax.ShapeDtypeStruct((ENS, TILE, SLIM), bf16),
            jax.ShapeDtypeStruct((ENS, ENS), f32),
        ),
        in_specs=[anyspace, anyspace, anyspace, vmem, anyspace, vmem, vmem],
        out_specs=(anyspace, anyspace, vmem),
        scratch_shapes=[
            pltpu.VMEM((ND, 2, 256, 512), bf16),
            pltpu.VMEM((ND, 2, 512, 512), bf16),
            pltpu.VMEM((ND, 256, 256), bf16),
            pltpu.VMEM((2, ND, 1024, 512), bf16),
            pltpu.VMEM((2, 1024, 512), f32),
            pltpu.VMEM((ND, ROWS, 256), f32),
            pltpu.VMEM((ND, ROWS, 256), f32),
            pltpu.VMEM((NM, ROWS, 256), f32),
            pltpu.VMEM((ENS, 2560), bf16),
            pltpu.VMEM((ENS, 2560), bf16),
            pltpu.VMEM((ENS + 8, ENS), f32),
            pltpu.VMEM((ND - 1, ENS + 8, ENS), f32),
            pltpu.SemaphoreType.DMA((3, ND)),
            pltpu.SemaphoreType.DMA((3, ND)),
            pltpu.SemaphoreType.DMA,
            pltpu.SemaphoreType.DMA,
            pltpu.SemaphoreType.DMA((LAST_TILES,)),
            pltpu.SemaphoreType.DMA,
            pltpu.SemaphoreType.DMA((ND,)),
            pltpu.SemaphoreType.DMA((ND,)),
            pltpu.SemaphoreType.DMA((3,)),
            pltpu.SemaphoreType.DMA((3,)),
            pltpu.SemaphoreType.DMA((ND,)),
            pltpu.SemaphoreType.DMA((ND,)),
        ],
        compiler_params=pltpu.CompilerParams(collective_id=0, has_side_effects=True, vmem_limit_bytes=VMEM_LIMIT),
    )(first_weight, middle_weight, window, last_t, last_tiles, gain, observed)

    new_first, new_middle, new_last = pl.pallas_call(
        update_kernel,
        out_shape=(
            jax.ShapeDtypeStruct(first_weight.shape, bf16),
            jax.ShapeDtypeStruct(middle_weight.shape, bf16),
            jax.ShapeDtypeStruct(last_tiles.shape, bf16),
        ),
        in_specs=[anyspace, anyspace, vmem],
        out_specs=(anyspace, anyspace, anyspace),
        scratch_shapes=[
            pltpu.VMEM((ENS, TILE, WIDE + SLIM), bf16),
            pltpu.VMEM((ENS, TILE, SLIM), bf16),
            pltpu.VMEM((ENS * TILE, ENS * TILE), bf16),
            pltpu.VMEM((ENS * TILE, ENS * TILE), bf16),
            pltpu.VMEM((ENS, TILE, WIDE + SLIM), bf16),
            pltpu.VMEM((ENS, TILE, SLIM), bf16),
            pltpu.SemaphoreType.DMA((2,)),
            pltpu.SemaphoreType.DMA,
            pltpu.SemaphoreType.DMA,
            pltpu.SemaphoreType.DMA,
            pltpu.SemaphoreType.DMA,
            pltpu.SemaphoreType.DMA,
        ],
        compiler_params=pltpu.CompilerParams(collective_id=1, has_side_effects=True, vmem_limit_bytes=VMEM_LIMIT),
    )(theta, theta_last, mix_t)
    new_last = new_last.reshape(members_here, padded)[:, :per_member].reshape(last_weight.shape)
    return (new_first, new_middle, new_last)


def solution(mesh):
    in_specs = (
        P("dp", None),
        P("dp"),
        P("dp"),
        P(),
        P("member", None, "dp"),
        P("member", "dp", None),
        P("member", "dp", None),
    )
    out_specs = (P("member", None, "dp"), P("member", "dp", None), P("member", "dp", None))
    return jax.shard_map(
        on_device, mesh=mesh, in_specs=in_specs, out_specs=out_specs, check_vma=False
    )
```

time: 422 us -> 311 us (0.74); the launches traced: 416 us -> 311 us
  Pallas kernels: 0 us -> 291 us
  waiting for transfers between devices: 198 us -> 0 us
  starting transfers between devices: 44 us -> 0 us
  other arithmetic: 45.7 us -> 2 us
  local copies, waits for them, and re-layouts: 57.4 us -> 16.7 us
  blocking collectives: 38.3 us -> 0 us
  matrix products: 18 us -> 0 us
  between operations: 14.7 us -> 0.7 us
    pallas_call x0 -> x2, Pallas kernels: none -> 291 us  [the longest x1 154 us: on_device(): pl.pallas_call(forward_kernel, out_shape=(jax.ShapeDtypeStruct((ENS, TILE...]
    all_to_all x4 -> x0, waiting for transfers between devices: 152 us -> none  [the longest x2 150 us: side_by_side(): lax.all_to_all(both, axis, split_axis=split_dim, concat_axis=concat_dim,...]
    all_to_all x4 -> x0, starting transfers between devices: 43.9 us -> none  [the longest x2 19.1 us: side_by_side(): lax.all_to_all(both, axis, split_axis=split_dim, concat_axis=concat_dim,...]
    reduce_scatter x1 -> x0, waiting for transfers between devices: 31.2 us -> none  [on_device(): lax.psum_scatter(term.reshape(lax.axis_size('dp') * local_count, members_...]
    another operation x5 -> x1, other arithmetic: 22.9 us -> 0.63 us  [on_device(): jnp.stack([jnp.pad(turned[m], ((m * classes_total, ROWS - (m + 1) * class...]
    dot_general x7 -> x0, matrix products: 17.4 us -> none  [the longest x1 9.46 us: on_device(): jnp.einsum('jsk,jkh->sjh', hidden_one, middle_weight, preferred_element_t...]
    unnamed x28 -> x10, local copies, waits for them, and re-layouts: 27.9 us -> 10.5 us
    all_gather x1 -> x0, waiting for transfers between devices: 14.3 us -> none  [on_device(): every_member = lax.all_gather(scaled, 'member', axis=0, tiled=True)]
  transfers between devices with their start and end apart: 6 -> 0, of which waited for: 6 -> 0; matrix products, arithmetic and copies ran while one was open for 14% -> 0% of each run, Pallas kernels for 0% -> 0%
where the time goes in v1:
time: 311 us
  Pallas kernels  291 us (94%)
  local copies, waits for them, and re-layouts  16.7 us (5%)
    pallas_call x1, Pallas kernels, on_device(): pl.pallas_call(forward_kernel, out_shape=(jax.ShapeDtypeStruct((ENS, TILE...  154 us
    pallas_call x1, Pallas kernels, on_device(): pl.pallas_call(update_kernel, out_shape=(jax.ShapeDtypeStruct(first_weigh...  137 us
    unnamed x10, local copies, waits for them, and re-layouts  10.5 us

profile of v1, /device:TPU:1, one launch (start us, length us, event | category | flops | bytes accessed | tf_op | source)
XLA Modules:
  0.0 310.6 jit_solution(7862763905960010359)
XLA Ops:
  0.6 0.0 copy-start
  0.6 0.7 sqrt.3
  1.4 0.1 tile.10
  1.4 0.7 compare_select_fusion
  2.1 2.0 gather_fusion.1
  4.1 0.7 broadcast_in_dim.5.gain
  4.8 0.7 fusion.observed
  5.5 0.7 copy.18
  6.2 0.6 pad_maximum_fusion.last_t
  6.9 0.0 copy-done
  6.9 1.8 gather_fusion
  8.7 0.9 copy.12
  9.6 0.4 reshape.22
  10.0 0.6 copy.14
  10.6 154.3 %shard_map.94 = (bf16[128,16,1152]{2,1,0:T(8,128)(2,1)}, bf16[128,16,128]{2,1,0:T(8,128)(2,1)}, f32[128,128]{1,0:T(8,128)}) custom-call(bf16[2,256,512]{2,1,0:T(8,128)(2,1)} %first.1, bf16[2,512,2048]{2,1,0:T(8,128)(2,1)} %middle.1, bf16[256,256]{1,0:T(8,128)(2,1)} %gather_fusion, bf16[2,24,512]{2,1,0:T(8,128)(2,1)} %pad_maximum_fusion.last_t, ...), custom_call_target="tpu_custom_call" | custom-call | tf_op jit(solution)/shard_map/pallas_call | solution.py:439
  165.0 136.8 %shard_map.95 = (bf16[2,256,512]{2,1,0:T(8,128)(2,1)}, bf16[2,512,2048]{2,1,0:T(8,128)(2,1)}, bf16[2,3,16,128]{3,2,1,0:T(8,128)(2,1)}) custom-call(bf16[128,16,1152]{2,1,0:T(8,128)(2,1)} %get-tuple-element.9.theta_hbm, bf16[128,16,128]{2,1,0:T(8,128)(2,1)} %get-tuple-element.10.theta_last_hbm, f32[128,128]{1,0:T(8,128)} %get-tuple-element.11.mix_t), custom_call_target="tpu_custom_call" | custom-call | tf_op jit(solution)/shard_map/pallas_call | solution.py:477
  301.8 0.8 copy.19
  302.6 0.5 reshape.25
  303.2 0.8 copy.13
  303.9 1.9 copy.22
  305.8 4.8 %copy.23 = bf16[2,512,2048]{2,1,0:T(8,128)(2,1)} copy(bf16[2,512,2048]{2,1,0:T(8,128)(2,1)} %get-tuple-element.26) | data formatting | bytes 8388608
  (8 shorter events, 0.1 us)
Async XLA Ops:
  0.6 6.2 %copy-start = (bf16[512,256]{1,0:T(8,128)(2,1)S(1)}, bf16[512,256]{1,0:T(8,128)(2,1)}, u32[]{:S(2)}) copy-start(bf16[512,256]{1,0:T(8,128)(2,1)} %param.7) | copy-start | bytes 786436

commit v2 on v0

v2 whole, which is shorter than its diff:
```python
import functools

import jax
import jax.numpy as jnp
from jax import lax
from jax.experimental import pallas as pl
from jax.experimental.pallas import tpu as pltpu
from jax.sharding import PartitionSpec as P

F_IN = 256
H = 2048
MESH = pl.DeviceIdType.MESH
NM = 64
ND = 4
ENS = 128
CLASSES = 10
TILE = 16
WIDE = 1024
SLIM = 128
VMEM_LIMIT = 60 * 1024 * 1024
OVER_LAST = (((1,), (1,)), ((), ()))
OVER_FIRST = (((0,), (0,)), ((), ()))


def dot32(a, b, dims=(((1,), (0,)), ((), ()))):
    return lax.dot_general(a, b, dims, preferred_element_type=jnp.float32)


def iota(shape, dim):
    return lax.broadcasted_iota(jnp.int32, shape, dim)


def middle_block(p):
    return pl.ds(pl.multiple_of((p // 2) * TILE, TILE), TILE), pl.ds(pl.multiple_of((p % 2) * WIDE, WIDE), WIDE)


def first_block(p):
    return pl.ds(pl.multiple_of((p // 4) * TILE, TILE), TILE), pl.ds(pl.multiple_of((p % 4) * SLIM, SLIM), SLIM)


def pair(p):
    return pl.ds(pl.multiple_of(2 * p, 2), 2)


def swing(turn):
    up = (turn + 1) // 2
    out = (turn % 2) * up + (1 - turn % 2) * (8 - up)
    far = (7 - turn) // 7
    return (out * (1 - far) + 4 * far - 4 * (turn // 7)) % 8


def whole_wait(ref, sem):
    pltpu.make_async_copy(ref, ref, sem).wait()


def spd_inverse(system):
    size = system.shape[0]
    group = 8
    sub = iota((group, size), 0)
    lane = iota((group, size), 1)
    lanes = iota((size - group, size), 1)

    def one_round(_, a):
        panel = a[:group, :]
        for k in range(group):
            row = panel[k:k + 1, :]
            col = panel[:, k:k + 1]
            pivot = 1.0 / row[:, k:k + 1]
            row = jnp.where(lane[:1] == k, pivot, row * pivot)
            panel = jnp.where(sub == k, row, jnp.where(lane == k, 0.0, panel) - col * row)
        below = jnp.where(lanes < group, 0.0, a[group:, :])
        for k in range(group):
            below = below - a[group:, k:k + 1] * panel[k:k + 1, :]
        turned = jnp.concatenate([below, panel], axis=0)
        return pltpu.roll(turned, size - group, 1)

    return lax.fori_loop(0, size // group, one_round, system)


def member_of_slot(i):
    return (i % 8) * 16 + ((i // 8) % 4) * 4 + i // 32


def kernel(
    first, middle, pool, labels, rows_picked, last, variance,
    new_first, new_middle, new_last,
    theta, theta_last, wf, mc, xw, h1, acc, lt, last_rows, part, part_in, every, hi_part, lo_part, gram, gram_in,
    mix_hi, mix_lo, wide_hi, wide_lo, out, out_last,
    x_send, x_recv, f_send, f_recv, m_send, m_recv, t_send, t_recv,
    a_send, a_recv, l_send, l_recv, p_send, p_recv, s_send, s_recv, g_send, g_recv,
    u_send, um_recv, uf_recv, ul_send, ul_recv,
):
    bf16, f32 = jnp.bfloat16, jnp.float32
    me, y = lax.axis_index("member"), lax.axis_index("dp")
    z, x, core = me // 8, (me // 2) % 4, me % 2
    chip = me - core
    barrier = pltpu.get_barrier_semaphore()
    for c in range(2):
        for d in range(1, ND):
            pl.semaphore_signal(barrier, inc=1, device_id=(chip + c, (y + d) % ND), device_id_type=MESH)

    def greet(i, carry):
        pl.semaphore_signal(barrier, inc=1, device_id=((me + i) % NM, y), device_id_type=MESH)
        return carry

    lax.fori_loop(1, NM, greet, 0)

    picked = (iota((512, 256), 0) == rows_picked[...]).astype(bf16)
    xw[0] = dot32(picked, pool[...], OVER_FIRST).astype(bf16)
    target = dot32((iota((16, 512), 0) == labels[...]).astype(bf16), picked)
    turn_classes = (iota((16, CLASSES), 0) == iota((16, CLASSES), 1)).astype(bf16)
    for m in range(2):
        last_rows[m] = dot32(turn_classes, last[m], OVER_LAST).astype(bf16)
    spread_var = jnp.ones((16, 128), f32)
    for c in range(CLASSES):
        spread_var = jnp.where(iota((16, 128), 0) == c, variance[c], spread_var)
    gain = 1.0 / jnp.sqrt(spread_var)
    observed = jnp.where(core == 0, target[:, :128], target[:, 128:]) * gain

    pl.semaphore_wait(barrier, NM - 1 + 2 * (ND - 1))

    def x_copy(d):
        return pltpu.make_async_remote_copy(
            src_ref=xw.at[0], dst_ref=xw.at[d], send_sem=x_send.at[d], recv_sem=x_recv.at[d],
            device_id=(me, (y - d) % ND), device_id_type=MESH,
        )

    def give(src, dst, send_sem, recv_sem, c, t, waiting=False):
        away = (t != y) | (c != core)

        @pl.when(away)
        def _():
            copy = pltpu.make_async_remote_copy(
                src_ref=src, dst_ref=dst, send_sem=send_sem, recv_sem=recv_sem, device_id=(chip + c, t), device_id_type=MESH
            )
            if waiting:
                copy.wait_send()
            else:
                copy.start()

        if not waiting:
            @pl.when(jnp.logical_not(away))
            def _():
                pltpu.make_async_copy(src, dst, recv_sem).start()

    def give_first(waiting):
        for m in range(2):
            t = 2 * core + m
            slot = (y - t) % ND
            for c in range(2):
                give(first.at[m], wf.at[slot], f_send.at[m, c], f_recv.at[slot], c, t, waiting)
            give(last_rows.at[m], lt.at[y % 2], t_send.at[m], t_recv.at[y % 2], y // 2, t, waiting)

    def give_middle(waiting):
        for half in range(2):
            for m in range(2):
                t = 2 * core + m
                slot = (y - t) % ND
                for c in range(2):
                    src = middle.at[m, :, pl.ds(c * 1024 + half * 512, 512)]
                    give(src, mc.at[half, slot], m_send.at[half, m, c], m_recv.at[half, slot], c, t, waiting)

    for d in (2, 1, 3):
        x_copy(d).start()
    give_first(False)
    give_middle(False)

    def exchange(p, remote):
        mr, mcol = middle_block(p)
        fr, fcol = first_block(p)
        jobs = (
            (middle.at[:, mr, mcol], theta.at[pair(me), :, pl.ds(0, WIDE)]),
            (first.at[:, fr, fcol], theta.at[pair(me), :, pl.ds(WIDE, SLIM)]),
        )
        for src, dst in jobs:
            if remote:
                pltpu.make_async_remote_copy(
                    src_ref=src, dst_ref=dst, send_sem=a_send, recv_sem=a_recv, device_id=(p, y), device_id_type=MESH
                ).start()
            else:
                pltpu.make_async_copy(src, dst, a_recv).start()

    def send_one(step, carry):
        p = ((z + swing(step % 8)) % 8) * 8 + (me % 8 + step // 8) % 8

        @pl.when(p != me)
        def _():
            exchange(p, True)

        @pl.when(p == me)
        def _():
            exchange(p, False)

        return carry

    lax.fori_loop(0, NM, send_one, 0)
    for t in range(4):
        owner = 3 + 17 * t
        src = last_rows.at[:, :, pl.ds(t * 128, 128)]

        @pl.when(me == owner)
        def _():
            pltpu.make_async_copy(src, theta_last.at[pair(me)], l_recv).start()

        @pl.when(me != owner)
        def _():
            pltpu.make_async_remote_copy(
                src_ref=src, dst_ref=theta_last.at[pair(me)], send_sem=l_send.at[t], recv_sem=l_recv,
                device_id=(owner, y), device_id_type=MESH,
            ).start()

    in_scale = F_IN ** (-0.5)
    hid_scale = H ** (-0.5)
    order = (0, 1, 3, 2)
    for d in (1, 3, 2):
        x_copy(d).wait_recv()
    for d in order:
        whole_wait(wf.at[d], f_recv.at[d])

        def rows_one(i, carry, d=d):
            rows = pl.ds(pl.multiple_of(i * 256, 256), 256)
            h1[d, rows, :] = jnp.tanh(dot32(xw[i], wf[d]) * in_scale).astype(bf16)
            return carry

        lax.fori_loop(0, 4, rows_one, 0)
    for s in range(2):
        whole_wait(lt.at[s], t_recv.at[s])
    for half in range(2):
        for n, d in enumerate(order):
            whole_wait(mc.at[half, d], m_recv.at[half, d])

            def rows_two(i, carry, d=d, n=n, half=half):
                rows = pl.ds(pl.multiple_of(i * 256, 256), 256)
                term = dot32(h1[d, rows, :], mc[half, d])
                if n == 0:
                    acc[rows, :] = term
                elif n < ND - 1:
                    acc[rows, :] += term
                else:
                    h2 = jnp.tanh((acc[rows, :] + term) * hid_scale).astype(bf16)
                    here = dot32(lt[half], h2, OVER_LAST)
                    for c in range(2):
                        piece = here[:, c * 128:(c + 1) * 128]
                        if half == 0:
                            part[i, c] = piece
                        else:
                            part[i, c] += piece
                return carry

            lax.fori_loop(0, 4, rows_two, 0)

    mine = core * ND + y
    def part_copy(d, c):
        return pltpu.make_async_remote_copy(
            src_ref=part.at[d, c], dst_ref=part_in.at[mine], send_sem=p_send, recv_sem=p_recv,
            device_id=(chip + c, (y + d) % ND), device_id_type=MESH,
        )

    for c in range(2):
        for d in range(ND):
            if d == 0:
                @pl.when(core != c)
                def _():
                    part_copy(0, c).start()

                @pl.when(core == c)
                def _():
                    part_in[mine] = part[0, c]
            else:
                part_copy(d, c).start()
    whole_wait(part_in.at[pl.ds(0, 7)], p_recv)
    scaled = [((part_in[s] + part_in[ND + s]) * hid_scale * gain)[:CLASSES] for s in range(ND)]
    every[x * 8 + z] = jnp.concatenate(scaled, axis=0)

    def spread(phase, first_slot, count, p):
        slots = every.at[pl.ds(first_slot, count)]
        return pltpu.make_async_remote_copy(
            src_ref=slots, dst_ref=slots, send_sem=s_send.at[phase], recv_sem=s_recv.at[phase],
            device_id=(p, y), device_id_type=MESH,
        )

    for i in (4, 3, 5, 2, 6, 1, 7):
        spread(0, x * 8 + z, 1, ((z + i) % 8) * 8 + x * 2 + core).start()
    whole_wait(every.at[pl.ds(0, 7)], s_recv.at[0])
    for i in (2, 1, 3):
        spread(1, pl.multiple_of(x * 8, 8), 8, z * 8 + ((x + i) % 4) * 2 + core).start()
    whole_wait(every.at[pl.ds(0, 24)], s_recv.at[1])

    pull = jnp.zeros((ENS, 128), f32)
    for c in range(CLASSES):
        values = jnp.concatenate([every[:, s * CLASSES + c, :] for s in range(ND)], axis=0)
        center = jnp.mean(values, axis=0, keepdims=True)
        anomaly = values - center
        upper = anomaly.astype(bf16)
        hi_part[:, c * 128:(c + 1) * 128] = upper
        lo_part[:, c * 128:(c + 1) * 128] = (anomaly - upper.astype(f32)).astype(bf16)
        pull = pull + anomaly * (observed[c:c + 1, :] - center)
    squares = dot32(hi_part[...], hi_part[...], OVER_LAST)
    crossed = dot32(hi_part[...], lo_part[...], OVER_LAST)
    gram[:ENS, :] = squares + (crossed + crossed.T)
    drive_tall = jnp.broadcast_to(jnp.sum(pull, axis=1, keepdims=True), (ENS, ENS))
    gram[ENS:, :] = drive_tall.T[:8, :]

    def gram_copy(k):
        dc, dy = k // ND, k % ND
        return pltpu.make_async_remote_copy(
            src_ref=gram, dst_ref=gram_in.at[k - 1], send_sem=g_send, recv_sem=g_recv,
            device_id=(chip + (core + dc) % 2, (y + dy) % ND), device_id_type=MESH,
        )

    for k in (2, 6, 1, 3, 5, 7, 4):
        gram_copy(k).start()
    whole_wait(gram_in, g_recv)
    summed = gram[...]
    for k in range(7):
        summed = summed + gram_in[k]
    diagonal = iota((ENS, ENS), 0) == iota((ENS, ENS), 1)
    inverse = spd_inverse(summed[:ENS] + jnp.where(diagonal, float(ENS), 0.0))
    lift = jnp.sum(inverse * summed[ENS:ENS + 1], axis=1, keepdims=True)
    mix_t = (
        float(ENS) * (inverse - jnp.mean(inverse, axis=0, keepdims=True))
        + (lift - jnp.mean(lift, axis=0, keepdims=True))
        + 1.0 / ENS
    )
    upper = mix_t.astype(bf16)
    size = ENS * TILE
    natural = (iota((ENS, ENS), 0) == member_of_slot(iota((ENS, ENS), 1))).astype(bf16)
    mix_hi[...] = dot32(natural, upper).astype(bf16)
    mix_lo[...] = dot32(natural, (mix_t - upper.astype(f32)).astype(bf16)).astype(bf16)

    whole_wait(theta, a_recv)
    is_owner = (me - 3) % 17 == 0
    my_tile = pl.ds(pl.multiple_of(((me + 14) // 17 - 1) % 4 * 128, 128), 128)

    @pl.when(is_owner)
    def _():
        whole_wait(theta_last, l_recv)

    mr, mcol = middle_block(me)
    fr, fcol = first_block(me)

    def results(slot, p, remote):
        jobs = (
            (out.at[pair(slot), :, pl.ds(0, WIDE)], new_middle.at[:, mr, mcol], um_recv),
            (out.at[pair(slot), :, pl.ds(WIDE, SLIM)], new_first.at[:, fr, fcol], uf_recv),
        )
        for src, dst, sem in jobs:
            if remote:
                pltpu.make_async_remote_copy(
                    src_ref=src, dst_ref=dst, send_sem=u_send, recv_sem=sem, device_id=(p, y), device_id_type=MESH
                ).start()
            else:
                pltpu.make_async_copy(src, dst, sem).start()

        @pl.when(is_owner)
        def _():
            src, dst = out_last.at[pair(slot)], new_last.at[:, :, my_tile]
            if remote:
                pltpu.make_async_remote_copy(
                    src_ref=src, dst_ref=dst, send_sem=ul_send, recv_sem=ul_recv, device_id=(p, y), device_id_type=MESH
                ).start()
            else:
                pltpu.make_async_copy(src, dst, ul_recv).start()

    block = 256

    def one_block(b, carry):
        low = (me % 8 + b) % 8
        k = iota((block, ENS), 0) // TILE
        member = ((k // 2) * 8 + low) * 2 + k % 2
        choose = (member == member_of_slot(iota((block, ENS), 1))).astype(bf16)
        repeat = (iota((ENS, size), 0) == iota((ENS, size), 1) // TILE).astype(bf16)
        keep = (iota((block, size), 0) % TILE) == (iota((block, size), 1) % TILE)
        for source, wide in ((mix_hi, wide_hi), (mix_lo, wide_lo)):
            tall = dot32(choose, source[...], OVER_LAST).astype(bf16)
            wide[...] = jnp.where(keep, dot32(tall, repeat), 0.0).astype(bf16)
        flat = theta[...].reshape(size, WIDE + SLIM)
        mixed = dot32(wide_hi[...], flat) + dot32(wide_lo[...], flat)
        here = pl.ds(pl.multiple_of(b * 16, 16), 16)
        out[here] = mixed.astype(bf16).reshape(16, TILE, WIDE + SLIM)

        @pl.when(is_owner)
        def _():
            tiles = theta_last[...].reshape(size, SLIM)
            done = dot32(wide_hi[...], tiles) + dot32(wide_lo[...], tiles)
            out_last[here] = done.astype(bf16).reshape(16, TILE, SLIM)

        def send_result(turn, inner):
            there = (z + swing(turn)) % 8
            p = there * 8 + low
            slot = b * 8 + there

            @pl.when(p != me)
            def _():
                results(slot, p, True)

            @pl.when(p == me)
            def _():
                results(slot, p, False)

            return inner

        lax.fori_loop(0, 8, send_result, 0)
        return carry

    lax.fori_loop(0, 8, one_block, 0)

    for d in range(1, ND):
        x_copy(d).wait_send()
    give_first(True)
    give_middle(True)
    rest = pl.ds(0, ENS - 2)
    whole_wait(theta.at[rest], a_send)
    for t in range(4):
        @pl.when(me != 3 + 17 * t)
        def _():
            whole_wait(last_rows.at[:, :, pl.ds(t * 128, 128)], l_send.at[t])
    whole_wait(part_in.at[pl.ds(0, 7)], p_send)
    whole_wait(every.at[pl.ds(0, 7)], s_send.at[0])
    whole_wait(every.at[pl.ds(0, 24)], s_send.at[1])
    whole_wait(gram_in, g_send)
    whole_wait(new_middle, um_recv)
    whole_wait(new_first, uf_recv)
    whole_wait(new_last, ul_recv)
    whole_wait(out.at[rest], u_send)

    @pl.when(is_owner)
    def _():
        whole_wait(out_last.at[rest], ul_send)


def on_device(
    feature_pool, labels, sample_rows, noise_variance, first_weight, middle_weight, last_weight
):
    anyspace = pl.BlockSpec(memory_space=pl.ANY)
    vmem = pl.BlockSpec(memory_space=pltpu.VMEM)
    smem = pl.BlockSpec(memory_space=pltpu.SMEM)
    bf16, f32 = jnp.bfloat16, jnp.float32
    dma = pltpu.SemaphoreType.DMA
    new_first, new_middle, new_last = pl.pallas_call(
        kernel,
        out_shape=(
            jax.ShapeDtypeStruct(first_weight.shape, bf16),
            jax.ShapeDtypeStruct(middle_weight.shape, bf16),
            jax.ShapeDtypeStruct((2, TILE, 512), bf16),
        ),
        in_specs=[anyspace, anyspace, vmem, vmem, vmem, vmem, smem],
        out_specs=(anyspace, anyspace, anyspace),
        scratch_shapes=[
            pltpu.VMEM((ENS, TILE, WIDE + SLIM), bf16),
            pltpu.VMEM((ENS, TILE, SLIM), bf16),
            pltpu.VMEM((ND, 256, 512), bf16),
            pltpu.VMEM((2, ND, 512, 512), bf16),
            pltpu.VMEM((ND, 256, 256), bf16),
            pltpu.VMEM((ND, 1024, 512), bf16),
            pltpu.VMEM((1024, 512), f32),
            pltpu.VMEM((2, TILE, 512), bf16),
            pltpu.VMEM((2, TILE, 512), bf16),
            pltpu.VMEM((ND, 2, 16, 128), f32),
            pltpu.VMEM((2 * ND, 16, 128), f32),
            pltpu.VMEM((32, ND * CLASSES, 128), f32),
            pltpu.VMEM((ENS, CLASSES * 128), bf16),
            pltpu.VMEM((ENS, CLASSES * 128), bf16),
            pltpu.VMEM((ENS + 8, ENS), f32),
            pltpu.VMEM((7, ENS + 8, ENS), f32),
            pltpu.VMEM((ENS, ENS), bf16),
            pltpu.VMEM((ENS, ENS), bf16),
            pltpu.VMEM((256, ENS * TILE), bf16),
            pltpu.VMEM((256, ENS * TILE), bf16),
            pltpu.VMEM((ENS, TILE, WIDE + SLIM), bf16),
            pltpu.VMEM((ENS, TILE, SLIM), bf16),
            dma((ND,)), dma((ND,)),
            dma((2, 2)), dma((ND,)),
            dma((2, 2, 2)), dma((2, ND)),
            dma((2,)), dma((2,)),
            dma, dma,
            dma((4,)), dma,
            dma, dma,
            dma((2,)), dma((2,)),
            dma, dma,
            dma, dma, dma, dma, dma,
        ],
        compiler_params=pltpu.CompilerParams(collective_id=0, has_side_effects=True, vmem_limit_bytes=VMEM_LIMIT),
    )(
        first_weight, middle_weight, feature_pool, labels.reshape(1, -1), sample_rows.reshape(1, -1), last_weight,
        noise_variance,
    )
    new_last = jnp.swapaxes(new_last[:, :CLASSES, :], 1, 2)
    return (new_first, new_middle, new_last)


def solution(mesh):
    in_specs = (
        P("dp", None),
        P("dp"),
        P("dp"),
        P(),
        P("member", None, "dp"),
        P("member", "dp", None),
        P("member", "dp", None),
    )
    out_specs = (P("member", None, "dp"), P("member", "dp", None), P("member", "dp", None))
    return jax.shard_map(
        on_device, mesh=mesh, in_specs=in_specs, out_specs=out_specs, check_vma=False
    )
```

time: 422 us -> 279 us (0.66)
  Pallas kernels: 0 us -> 266 us
  waiting for transfers between devices: 198 us -> 0 us
  local copies, waits for them, and re-layouts: 57.4 us -> 9.64 us
  other arithmetic: 45.7 us -> 0 us
  starting transfers between devices: 44 us -> 0 us
  blocking collectives: 38.3 us -> 0 us
  matrix products: 18 us -> 0 us
  between operations: 14.7 us -> 0.64 us
    pallas_call x0 -> x1, Pallas kernels: none -> 266 us  [on_device(): pl.pallas_call(kernel, out_shape=(jax.ShapeDtypeStruct(first_weight.shape...]
    all_to_all x4 -> x0, waiting for transfers between devices: 152 us -> none  [the longest x2 150 us: side_by_side(): lax.all_to_all(both, axis, split_axis=split_dim, concat_axis=concat_dim,...]
    all_to_all x4 -> x0, starting transfers between devices: 43.9 us -> none  [the longest x2 19.1 us: side_by_side(): lax.all_to_all(both, axis, split_axis=split_dim, concat_axis=concat_dim,...]
    reduce_scatter x1 -> x0, waiting for transfers between devices: 31.2 us -> none  [on_device(): lax.psum_scatter(term.reshape(lax.axis_size('dp') * local_count, members_...]
    another operation x5 -> x0, other arithmetic: 22.9 us -> none  [the longest x3 12.4 us: on_device(): factor = jnp.linalg.cholesky(system)]
    unnamed x28 -> x4, local copies, waits for them, and re-layouts: 27.9 us -> 8.88 us
    dot_general x7 -> x0, matrix products: 17.4 us -> none  [the longest x1 9.46 us: on_device(): jnp.einsum('jsk,jkh->sjh', hidden_one, middle_weight, preferred_element_t...]
    all_gather x1 -> x0, waiting for transfers between devices: 14.3 us -> none  [on_device(): every_member = lax.all_gather(scaled, 'member', axis=0, tiled=True)]
  transfers between devices with their start and end apart: 6 -> 0, of which waited for: 6 -> 0; matrix products, arithmetic and copies ran while one was open for 14% -> 0% of each run, Pallas kernels for 0% -> 0%
where the time goes in v2:
time: 279 us; the launch traced here: 276 us
  Pallas kernels  266 us (95%)
  local copies, waits for them, and re-layouts  9.64 us (3%)
    pallas_call x1, Pallas kernels, on_device(): pl.pallas_call(kernel, out_shape=(jax.ShapeDtypeStruct(first_weight.shape...  266 us
    unnamed x4, local copies, waits for them, and re-layouts  8.88 us

profile of v2, /device:TPU:1, one launch (start us, length us, event | category | flops | bytes accessed | tf_op | source)
XLA Modules:
  0.0 276.2 jit_solution(4524799568475201935)
XLA Ops:
  0.6 1.6 copy.10.last
  2.2 265.9 %shard_map.94 = (bf16[2,256,512]{2,1,0:T(8,128)(2,1)}, bf16[2,512,2048]{2,1,0:T(8,128)(2,1)}, bf16[2,16,512]{2,1,0:T(8,128)(2,1)}) custom-call(bf16[2,256,512]{2,1,0:T(8,128)(2,1)} %first.1, bf16[2,512,2048]{2,1,0:T(8,128)(2,1)} %middle.1, bf16[512,256]{1,0:T(8,128)(2,1)} %pool.1, s32[1,512]{1,0:T(1,128)} %bitcast.4, s32[1,256]{1,0:T(1,128)} %bitcast.5, ...), custom_call_target="tpu_custom_call" | custom-call | tf_op jit(solution)/shard_map/pallas_call | solution.py:440
  268.2 0.8 slice_bitcast_fusion
  268.9 0.6 copy.11
  269.6 1.9 copy.14
  271.4 4.8 %copy.15 = bf16[2,512,2048]{2,1,0:T(8,128)(2,1)} copy(bf16[2,512,2048]{2,1,0:T(8,128)(2,1)} %get-tuple-element.16) | data formatting | bytes 8388608

commit v3 on v2

--- a/solution.py
+++ b/solution.py
@@ -14,6 +14,7 @@
 ND = 4
 ENS = 128
 CLASSES = 10
+CUTS = (40, 40, 40, 56)
 TILE = 16
 WIDE = 1024
 SLIM = 128
@@ -62,12 +63,18 @@
 
     def one_round(_, a):
         panel = a[:group, :]
-        for k in range(group):
-            row = panel[k:k + 1, :]
-            col = panel[:, k:k + 1]
-            pivot = 1.0 / row[:, k:k + 1]
-            row = jnp.where(lane[:1] == k, pivot, row * pivot)
-            panel = jnp.where(sub == k, row, jnp.where(lane == k, 0.0, panel) - col * row)
+        for k in range(0, group, 2):
+            one, two = panel[k:k + 1, :], panel[k + 1:k + 2, :]
+            col_one, col_two = panel[:, k:k + 1], panel[:, k + 1:k + 2]
+            at_one, at_two = lane == k, lane == k + 1
+            p, q = one[:, k:k + 1], one[:, k + 1:k + 2]
+            r, t = two[:, k:k + 1], two[:, k + 1:k + 2]
+            scale = 1.0 / (p * t - q * r)
+            one = jnp.where(at_one[:1], 1.0, jnp.where(at_two[:1], 0.0, one))
+            two = jnp.where(at_one[:1], 0.0, jnp.where(at_two[:1], 1.0, two))
+            one, two = (t * one - q * two) * scale, (p * two - r * one) * scale
+            rest = jnp.where(at_one | at_two, 0.0, panel) - col_one * one - col_two * two
+            panel = jnp.where(sub == k, one, jnp.where(sub == k + 1, two, rest))
         below = jnp.where(lanes < group, 0.0, a[group:, :])
         for k in range(group):
             below = below - a[group:, k:k + 1] * panel[k:k + 1, :]
@@ -108,9 +115,10 @@
     picked = (iota((512, 256), 0) == rows_picked[...]).astype(bf16)
     xw[0] = dot32(picked, pool[...], OVER_FIRST).astype(bf16)
     target = dot32((iota((16, 512), 0) == labels[...]).astype(bf16), picked)
-    turn_classes = (iota((16, CLASSES), 0) == iota((16, CLASSES), 1)).astype(bf16)
+    by_class = [last[c].astype(f32) for c in range(CLASSES)]
     for m in range(2):
-        last_rows[m] = dot32(turn_classes, last[m], OVER_LAST).astype(bf16)
+        rows = [v[m:m + 1, :] for v in by_class] + [jnp.zeros((16 - CLASSES, 512), f32)]
+        last_rows[m] = jnp.concatenate(rows, axis=0).astype(bf16)
     spread_var = jnp.ones((16, 128), f32)
     for c in range(CLASSES):
         spread_var = jnp.where(iota((16, 128), 0) == c, variance[c], spread_var)
@@ -181,7 +189,8 @@
                 pltpu.make_async_copy(src, dst, a_recv).start()
 
     def send_one(step, carry):
-        p = ((z + swing(step % 8)) % 8) * 8 + (me % 8 + step // 8) % 8
+        turn = (step // 8 + 2) % 8
+        p = ((z + swing(step % 8)) % 8) * 8 + ((x + turn // 2) % 4) * 2 + (core + turn) % 2
 
         @pl.when(p != me)
         def _():
@@ -193,7 +202,10 @@
 
         return carry
 
-    lax.fori_loop(0, NM, send_one, 0)
+    def send_some(first_step, last_step):
+        lax.fori_loop(first_step, last_step, send_one, 0)
+
+    send_some(0, CUTS[0])
     for t in range(4):
         owner = 3 + 17 * t
         src = last_rows.at[:, :, pl.ds(t * 128, 128)]
@@ -268,6 +280,7 @@
                     part_in[mine] = part[0, c]
             else:
                 part_copy(d, c).start()
+    send_some(CUTS[0], CUTS[1])
     whole_wait(part_in.at[pl.ds(0, 7)], p_recv)
     scaled = [((part_in[s] + part_in[ND + s]) * hid_scale * gain)[:CLASSES] for s in range(ND)]
     every[x * 8 + z] = jnp.concatenate(scaled, axis=0)
@@ -281,9 +294,11 @@
 
     for i in (4, 3, 5, 2, 6, 1, 7):
         spread(0, x * 8 + z, 1, ((z + i) % 8) * 8 + x * 2 + core).start()
+    send_some(CUTS[1], CUTS[2])
     whole_wait(every.at[pl.ds(0, 7)], s_recv.at[0])
     for i in (2, 1, 3):
         spread(1, pl.multiple_of(x * 8, 8), 8, z * 8 + ((x + i) % 4) * 2 + core).start()
+    send_some(CUTS[2], CUTS[3])
     whole_wait(every.at[pl.ds(0, 24)], s_recv.at[1])
 
     pull = jnp.zeros((ENS, 128), f32)
@@ -310,6 +325,7 @@
 
     for k in (2, 6, 1, 3, 5, 7, 4):
         gram_copy(k).start()
+    send_some(CUTS[3], NM)
     whole_wait(gram_in, g_recv)
     summed = gram[...]
     for k in range(7):
@@ -482,7 +498,7 @@
         ],
         compiler_params=pltpu.CompilerParams(collective_id=0, has_side_effects=True, vmem_limit_bytes=VMEM_LIMIT),
     )(
-        first_weight, middle_weight, feature_pool, labels.reshape(1, -1), sample_rows.reshape(1, -1), last_weight,
+        first_weight, middle_weight, feature_pool, labels.reshape(1, -1), sample_rows.reshape(1, -1), jnp.transpose(last_weight, (2, 0, 1)),
         noise_variance,
     )
     new_last = jnp.swapaxes(new_last[:, :CLASSES, :], 1, 2)

time: 279 us -> 255 us (0.914)
  Pallas kernels: 266 us -> 245 us
    pallas_call x1, Pallas kernels: 266 us -> 245 us  [on_device(): pl.pallas_call(kernel, out_shape=(jax.ShapeDtypeStruct(first_weight.shape...]
    unnamed x4 -> x3, local copies, waits for them, and re-layouts: 8.88 us -> 7.28 us
where the time goes in v3:
time: 255 us; the launch traced here: 253 us
  Pallas kernels  245 us (96%)
  local copies, waits for them, and re-layouts  8.04 us (3%)
    pallas_call x1, Pallas kernels, on_device(): pl.pallas_call(kernel, out_shape=(jax.ShapeDtypeStruct(first_weight.shape...  245 us
    unnamed x3, local copies, waits for them, and re-layouts  7.28 us

profile of v3, /device:TPU:1, one launch (start us, length us, event | category | flops | bytes accessed | tf_op | source)
XLA Modules:
  0.0 253.3 jit_solution(1335030767976002255)
XLA Ops:
  0.6 244.6 %shard_map.94 = (bf16[2,256,512]{2,1,0:T(8,128)(2,1)}, bf16[2,512,2048]{2,1,0:T(8,128)(2,1)}, bf16[2,16,512]{2,1,0:T(8,128)(2,1)}) custom-call(bf16[2,256,512]{2,1,0:T(8,128)(2,1)} %first.1, bf16[2,512,2048]{2,1,0:T(8,128)(2,1)} %middle.1, bf16[512,256]{1,0:T(8,128)(2,1)} %pool.1, s32[1,512]{1,0:T(1,128)} %bitcast.6, s32[1,256]{1,0:T(1,128)} %bitcast.7, ...), custom_call_target="tpu_custom_call" | custom-call | tf_op jit(solution)/shard_map/pallas_call | solution.py:456
  245.2 0.8 slice_bitcast_fusion
  246.0 0.6 copy.10
  246.6 1.9 copy.13
  248.5 4.8 %copy.14 = bf16[2,512,2048]{2,1,0:T(8,128)(2,1)} copy(bf16[2,512,2048]{2,1,0:T(8,128)(2,1)} %get-tuple-element.16) | data formatting | bytes 8388608

commit v4 on v3

--- a/solution.py
+++ b/solution.py
@@ -443,6 +443,24 @@
     @pl.when(is_owner)
     def _():
         whole_wait(out_last.at[rest], ul_send)
+
+
+def settle(middle, first, settled_middle, settled_first, held_middle, held_first, in_sems, out_sems):
+    steps = []
+    for m in range(2):
+        for k in range(4):
+            at = (m, pl.ds(k * 128, 128))
+            steps.append((middle.at[at], held_middle.at[at], settled_middle.at[at], in_sems.at[m, k], out_sems.at[m, k]))
+        steps.append((first.at[m], held_first.at[m], settled_first.at[m], in_sems.at[m, 4], out_sems.at[m, 4]))
+    ins = [pltpu.make_async_copy(src, held, sem) for src, held, _, sem, _ in steps]
+    outs = [pltpu.make_async_copy(held, dst, sem) for _, held, dst, _, sem in steps]
+    for copy in ins:
+        copy.start()
+    for came, goes in zip(ins, outs):
+        came.wait()
+        goes.start()
+    for copy in outs:
+        copy.wait()
 
 
 def on_device(
@@ -501,6 +519,19 @@
         first_weight, middle_weight, feature_pool, labels.reshape(1, -1), sample_rows.reshape(1, -1), jnp.transpose(last_weight, (2, 0, 1)),
         noise_variance,
     )
+    new_middle, new_first = pl.pallas_call(
+        settle,
+        out_shape=(
+            jax.ShapeDtypeStruct(middle_weight.shape, bf16),
+            jax.ShapeDtypeStruct(first_weight.shape, bf16),
+        ),
+        in_specs=[anyspace, anyspace],
+        out_specs=(anyspace, anyspace),
+        scratch_shapes=[
+            pltpu.VMEM(middle_weight.shape, bf16), pltpu.VMEM(first_weight.shape, bf16), dma((2, 5)), dma((2, 5)),
+        ],
+        compiler_params=pltpu.CompilerParams(vmem_limit_bytes=VMEM_LIMIT),
+    )(new_middle, new_first)
     new_last = jnp.swapaxes(new_last[:, :CLASSES, :], 1, 2)
     return (new_first, new_middle, new_last)
 

time: 255 us -> 252 us (0.988)
  local copies, waits for them, and re-layouts: 8.04 us -> 0.64 us
    unnamed x3, local copies, waits for them, and re-layouts: 7.28 us -> 0.63 us
    pallas_call x0 -> x1, Pallas kernels: none -> 4.07 us  [on_device(): pl.pallas_call(settle, out_shape=(jax.ShapeDtypeStruct(middle_weight.shap...]
where the time goes in v4:
time: 252 us; the launch traced here: 248 us
  Pallas kernels  247 us (98%)
    pallas_call x1, Pallas kernels, on_device(): pl.pallas_call(kernel, out_shape=(jax.ShapeDtypeStruct(first_weight.shape...  243 us

profile of v4, /device:TPU:1, one launch (start us, length us, event | category | flops | bytes accessed | tf_op | source)
XLA Modules:
  0.0 248.2 jit_solution(7811157023906737298)
XLA Ops:
  0.6 242.8 %shard_map.94 = (bf16[2,256,512]{2,1,0:T(8,128)(2,1)}, bf16[2,512,2048]{2,1,0:T(8,128)(2,1)}, bf16[2,16,512]{2,1,0:T(8,128)(2,1)}) custom-call(bf16[2,256,512]{2,1,0:T(8,128)(2,1)} %first.1, bf16[2,512,2048]{2,1,0:T(8,128)(2,1)} %middle.1, bf16[512,256]{1,0:T(8,128)(2,1)} %pool.1, s32[1,512]{1,0:T(1,128)} %bitcast.6, s32[1,256]{1,0:T(1,128)} %bitcast.7, ...), custom_call_target="tpu_custom_call" | custom-call | tf_op jit(solution)/shard_map/pallas_call | solution.py:474
  243.4 0.0 copy-start
  243.4 4.1 %shard_map.95 = (bf16[2,512,2048]{2,1,0:T(8,128)(2,1)}, bf16[2,256,512]{2,1,0:T(8,128)(2,1)}) custom-call(bf16[2,512,2048]{2,1,0:T(8,128)(2,1)} %get-tuple-element.8.middle, bf16[2,256,512]{2,1,0:T(8,128)(2,1)} %get-tuple-element.9.first), custom_call_target="tpu_custom_call" | custom-call | tf_op jit(solution)/shard_map/pallas_call | solution.py:522
  247.5 0.0 copy-done
  247.6 0.6 copy.10
  (1 shorter events, 0.0 us)
Async XLA Ops:
  243.4 4.1 %copy-start = (bf16[2,16,512]{2,1,0:T(8,128)(2,1)S(1)}, bf16[2,16,512]{2,1,0:T(8,128)(2,1)}, u32[]{:S(2)}) copy-start(bf16[2,16,512]{2,1,0:T(8,128)(2,1)} %get-tuple-element.12) | copy-start | bytes 98308

commit v5 on v4

--- a/solution.py
+++ b/solution.py
@@ -14,7 +14,7 @@
 ND = 4
 ENS = 128
 CLASSES = 10
-CUTS = (40, 40, 40, 56)
+CUTS = (42, 42, 42, 56)
 TILE = 16
 WIDE = 1024
 SLIM = 128

time: 252 us -> 252 us (level)
  no operation moved by 1% of the time
where the time goes in v5:
time: 252 us; the launch traced here: 248 us
  Pallas kernels  247 us (98%)
    pallas_call x1, Pallas kernels, on_device(): pl.pallas_call(kernel, out_shape=(jax.ShapeDtypeStruct(first_weight.shape...  243 us

profile of v5, /device:TPU:1, one launch (start us, length us, event | category | flops | bytes accessed | tf_op | source)
XLA Modules:
  0.0 248.5 jit_solution(10541414365753301812)
XLA Ops:
  0.6 243.1 %shard_map.94 = (bf16[2,256,512]{2,1,0:T(8,128)(2,1)}, bf16[2,512,2048]{2,1,0:T(8,128)(2,1)}, bf16[2,16,512]{2,1,0:T(8,128)(2,1)}) custom-call(bf16[2,256,512]{2,1,0:T(8,128)(2,1)} %first.1, bf16[2,512,2048]{2,1,0:T(8,128)(2,1)} %middle.1, bf16[512,256]{1,0:T(8,128)(2,1)} %pool.1, s32[1,512]{1,0:T(1,128)} %bitcast.6, s32[1,256]{1,0:T(1,128)} %bitcast.7, ...), custom_call_target="tpu_custom_call" | custom-call | tf_op jit(solution)/shard_map/pallas_call | solution.py:474
  243.7 0.0 copy-start
  243.7 4.1 %shard_map.95 = (bf16[2,512,2048]{2,1,0:T(8,128)(2,1)}, bf16[2,256,512]{2,1,0:T(8,128)(2,1)}) custom-call(bf16[2,512,2048]{2,1,0:T(8,128)(2,1)} %get-tuple-element.8.middle, bf16[2,256,512]{2,1,0:T(8,128)(2,1)} %get-tuple-element.9.first), custom_call_target="tpu_custom_call" | custom-call | tf_op jit(solution)/shard_map/pallas_call | solution.py:522
  247.8 0.0 copy-done
  247.8 0.6 copy.10
  (1 shorter events, 0.0 us)
Async XLA Ops:
  243.7 4.1 %copy-start = (bf16[2,16,512]{2,1,0:T(8,128)(2,1)S(1)}, bf16[2,16,512]{2,1,0:T(8,128)(2,1)}, u32[]{:S(2)}) copy-start(bf16[2,16,512]{2,1,0:T(8,128)(2,1)} %get-tuple-element.12) | copy-start | bytes 98308
